TPU v7x, 32 devices: a whole 2x2x4 slice. The times are simulated.
32 devices in a mesh: tm: 2 (over y), space: 16 (over z, x, core).
Axes of the slice: x: 2, y: 2, z: 4, core: 2. Of those that a mesh axis runs over, the one named last changes fastest.
Arguments:
- fine_nodes: float32 [2, 3, 128, 128, 256], P('tm', None, 'space'), may hold values from -1.25 to 1.25
- fine_implicit: float32 [2, 3, 128, 128, 256], P('tm', None, 'space'), may hold values from -18 to 18
Outputs:
- new_nodes: float32 [2, 3, 128, 128, 256], P('tm', None, 'space')
- new_implicit: float32 [2, 2, 128, 128, 256], P('tm', None, 'space')
All inputs are finite; a program needn't handle non-finite values.
Results may differ from a plain program's by a relative error of at most 0.00014.
Values sent between devices are 32-bit elements; how exact they have to be, the bound alone decides.
A program may use at most 128 MiB of HBM per device.

v0:
```python
import math

import jax
import jax.numpy as jnp
import ml_dtypes
import numpy as np
from jax import lax
from jax.experimental import pallas as pl
from jax.experimental.pallas import tpu as pltpu
from jax.sharding import PartitionSpec as P

WEIGHTS = ((5.0 / 24.0, 1.0 / 3.0, -1.0 / 24.0), (-1.0 / 24.0, 1.0 / 3.0, 5.0 / 24.0))
EPS2 = 2.0
HIGHEST = lax.Precision.HIGHEST


def extended(block, sides, width):
    for axis, dim in sides:
        count = lax.axis_size(axis)
        forward = [(i, i + 1) for i in range(count - 1)]
        forward.append((count - 1, 0))
        backward = [(target, source) for source, target in forward]
        low = lax.ppermute(
            lax.slice_in_dim(block, block.shape[dim] - width, None, axis=dim), axis, forward
        )
        high = lax.ppermute(lax.slice_in_dim(block, 0, width, axis=dim), axis, backward)
        block = jnp.concatenate([low, block, high], axis=dim)
    return block


def passed_along(value, axis, steps):
    count = lax.axis_size(axis)
    leading, last = (max(0, -steps), min(count, count - steps))
    return lax.ppermute(value, axis, [(source, source + steps) for source in range(leading, last)])


def shifted(value, axis, steps):
    count = lax.axis_size(axis)
    pairs = [(source, (source + steps) % count) for source in range(count)]
    return lax.ppermute(value, axis, pairs)


def react(u):
    return u - u * u * u


def real_basis(size):
    rows = lax.broadcasted_iota(jnp.int32, (size, size), 0)
    cells = lax.broadcasted_iota(jnp.int32, (size, size), 1)
    half = size // 2
    freq = jnp.where(rows <= half, rows, rows - half)
    phase = (freq * cells % size).astype(jnp.float32) * (2.0 * math.pi / size)
    scale = jnp.where((rows == 0) | (rows == half), 1.0 / math.sqrt(size), math.sqrt(2.0 / size))
    return jnp.where(rows <= half, jnp.cos(phase), jnp.sin(phase)) * scale


def wave_square(index, size):
    half = size // 2
    freq = jnp.where(index <= half, index, index - half).astype(jnp.float32)
    kappa = freq * (2.0 * math.pi / size)
    return kappa * kappa


def interp_matrix(size):
    fine_rows = lax.broadcasted_iota(jnp.int32, (2 * size, size), 0)
    coarse_cols = lax.broadcasted_iota(jnp.int32, (2 * size, size), 1)
    base = fine_rows // 2
    odd = fine_rows % 2
    take_base = jnp.where(coarse_cols == base, jnp.where(odd == 0, 1.0, 0.5), 0.0)
    take_next = jnp.where((odd == 1) & (coarse_cols == (base + 1) % size), 0.5, 0.0)
    return (take_base + take_next).astype(jnp.float32)


def spectral_solve(rhs, basis_x, basis_y, basis_z, factor):
    planes, size_y, size_z = rhs.shape
    flat = jnp.dot(rhs.reshape(planes * size_y, size_z), basis_z.T, precision=HIGHEST)
    field = flat.reshape(planes, size_y, size_z)
    field = jnp.einsum("ky,xyz->kxz", basis_y, field, precision=HIGHEST)
    field = lax.all_to_all(field, "space", split_axis=0, concat_axis=1, tiled=True)
    field = jnp.einsum("kx,yxz->kyz", basis_x, field, precision=HIGHEST) * factor
    field = jnp.einsum("kx,kyz->xyz", basis_x, field, precision=HIGHEST)
    field = lax.all_to_all(field, "space", split_axis=0, concat_axis=1, tiled=True)
    field = jnp.matmul(basis_y.T, field, precision=HIGHEST)
    flat = jnp.dot(field.reshape(planes * size_y, size_z), basis_z, precision=HIGHEST)
    return flat.reshape(planes, size_y, size_z)


def pool_matrix(size):
    rows = lax.broadcasted_iota(jnp.int32, (size // 2, size), 0)
    cells = lax.broadcasted_iota(jnp.int32, (size // 2, size), 1)
    return jnp.where(cells // 2 == rows, 0.5, 0.0).astype(jnp.float32)


def restrict(stacked):
    k, a, b, c = stacked.shape
    planes = stacked.reshape(k, a // 2, 2, b, c)
    planes = 0.5 * (planes[:, :, 0] + planes[:, :, 1])
    half = jnp.einsum("kayz,cz->kayc", planes, pool_matrix(c), precision=HIGHEST)
    return jnp.matmul(pool_matrix(b), half, precision=HIGHEST)


def coarse_rate(stacked):
    padded = extended(stacked, (("space", 1),), 1)
    lap = padded[:, 2:] + padded[:, :-2]
    lap = lap + jnp.roll(stacked, -1, 2) + jnp.roll(stacked, 1, 2)
    lap = lap + jnp.roll(stacked, -1, 3) + jnp.roll(stacked, 1, 3)
    return EPS2 * ((lap - 6.0 * stacked) * 0.25) + react(stacked)


def spread(values, following, axis):
    middle = 0.5 * (values + following)
    both = jnp.stack([values, middle], axis=axis + 1)
    shape = list(values.shape)
    shape[axis] = shape[axis] * 2
    return both.reshape(shape)


def refine(stacked, upper):
    matrix_y = interp_matrix(stacked.shape[2])
    matrix_z = interp_matrix(stacked.shape[3])
    both = jnp.concatenate([stacked, upper], axis=1)
    both = jnp.einsum("kayc,zc->kayz", both, matrix_z, precision=HIGHEST)
    both = jnp.matmul(matrix_y, both, precision=HIGHEST)
    planes = stacked.shape[1]
    return spread(both[:, :planes], both[:, 1:], 1)


def coarse_sweep(start, rates, sums):
    first = start + 0.25 * (coarse_rate(start[None])[0] - rates[0]) + sums[0]
    second = first + 0.25 * (coarse_rate(first[None])[0] - rates[1]) + sums[1]
    return (first, second)


def on_device(fine_nodes, fine_implicit):
    nodes = fine_nodes[0]
    implicit = fine_implicit[0]
    planes, size_y, size_z = (nodes.shape[1], nodes.shape[2], nodes.shape[3])
    devices = lax.axis_size("space")
    size_x = planes * devices
    local_y = size_y // devices
    basis_x = real_basis(size_x)
    basis_y = real_basis(size_y)
    basis_z = real_basis(size_z)
    columns = lax.axis_index("space") * local_y + lax.iota(jnp.int32, local_y)
    lam = wave_square(lax.iota(jnp.int32, size_x), size_x)[:, None, None]
    lam = lam + wave_square(columns, size_y)[None, :, None]
    lam = lam + wave_square(lax.iota(jnp.int32, size_z), size_z)[None, None, :]
    factor = 1.0 / (1.0 + 0.5 * lam)
    explicit_old = react(nodes)
    rates_old = explicit_old + implicit
    values = [nodes[0]]
    terms = [implicit[0]]
    for m in range(2):
        w = WEIGHTS[m]
        quad = 0.5 * (w[0] * rates_old[0] + w[1] * rates_old[1] + w[2] * rates_old[2])
        rhs = (
            values[m] + 0.25 * (react(values[m]) - explicit_old[m]) - 0.25 * implicit[m + 1] + quad
        )
        solved = spectral_solve(rhs, basis_x, basis_y, basis_z, factor)
        values.append(solved)
        terms.append((solved - rhs) * 4.0)
    carried = passed_along(values[2], "tm", 1)
    fresh = jnp.stack(values)
    rates_new = react(fresh) + jnp.stack(terms)
    sums = restrict(
        jnp.stack(
            [
                0.5 * (w[0] * rates_new[0] + w[1] * rates_new[1] + w[2] * rates_new[2])
                for w in WEIGHTS
            ]
        )
    )
    coarse = restrict(fresh)
    rates_c = coarse_rate(coarse[:2])
    slot = lax.axis_index("tm")
    slices = lax.axis_size("tm")
    start = coarse[0]
    for section in range(slices - 1):
        first, second = coarse_sweep(start, rates_c, sums)
        received = passed_along(second, "tm", 1)
        start = jnp.where(slot == 0, coarse[0], received)
    first, second = coarse_sweep(start, rates_c, sums)
    delta = jnp.stack([first - coarse[1], second - coarse[2]])
    upper = shifted(delta[:, :1], "space", -1)
    corr = refine(delta, upper)
    fixed_one = values[1] + corr[0]
    fixed_two = values[2] + corr[1]
    late_delta, late_upper = passed_along((delta[1:], upper[1:]), "tm", 1)
    received_end = carried + refine(late_delta, late_upper)[0]
    head = jnp.where(slot == 0, nodes[0], received_end)
    return (jnp.stack([head, fixed_one, fixed_two])[None], jnp.stack([terms[1], terms[2]])[None])


BF16 = jnp.bfloat16
F32 = jnp.float32
MESH = pl.DeviceIdType.MESH
CHUNKS = 2
LANES = 128
GROUP = 8
V0, V1, V2, S0, S1 = range(5)


def host_basis(size):
    rows = np.arange(size)[:, None]
    cells = np.arange(size)[None, :]
    half = size // 2
    freq = np.where(rows <= half, rows, rows - half)
    phase = (freq * cells % size) * (2.0 * math.pi / size)
    scale = np.where((rows == 0) | (rows == half), 1.0 / math.sqrt(size), math.sqrt(2.0 / size))
    return np.where(rows <= half, np.cos(phase), np.sin(phase)) * scale


def two_parts(matrix):
    high = matrix.astype(np.float32).astype(ml_dtypes.bfloat16)
    low = (matrix - high.astype(np.float64)).astype(np.float32).astype(ml_dtypes.bfloat16)
    return jnp.asarray(np.stack([high, low]))


def split(value):
    high = value.astype(BF16)
    return high, (value - high.astype(F32)).astype(BF16)


def product(a, b):
    return jnp.dot(a, b, preferred_element_type=F32)


def left(matrix, value):
    high, low = split(value)
    return product(matrix[0], high) + (product(matrix[0], low) + product(matrix[1], high))


def right(value, matrix):
    high, low = split(value)
    return product(high, matrix[0]) + (product(low, matrix[0]) + product(high, matrix[1]))


def right_exact(value, matrix):
    high, low = split(value)
    return product(high, matrix[...]) + product(low, matrix[...])


def rate(value):
    size_y, size_z = value.shape[1:]
    mid = value[1:-1]
    lap = value[2:] + value[:-2]
    lap = lap + pltpu.roll(mid, 1, 1) + pltpu.roll(mid, size_y - 1, 1)
    lap = lap + pltpu.roll(mid, 1, 2) + pltpu.roll(mid, size_z - 1, 2)
    return EPS2 * ((lap - 6.0 * mid) * 0.25) + react(mid)


def kernel(
    nodes, implicit, bz, bzt, bx, bxt, by, byt, pz, iz,
    out_n, out_i,
    send_a, recv_a, send_b, recv_b, passed, factor, pool, ext, va, vb, delta, rows, grid,
    a2a_send, a2a_recv, halo_send, halo_recv, time_send, time_recv,
):
    slot = lax.axis_index("tm")
    me = lax.axis_index("space")
    devices = lax.axis_size("space")
    planes, size_y, size_z = nodes.shape[2:]
    size_x = planes * devices
    block = planes * GROUP

    barrier = pltpu.get_barrier_semaphore()

    def greet(k, carry):
        pl.semaphore_signal(
            barrier, inc=1, device_id=(slot, lax.rem(me + k, devices)), device_id_type=MESH
        )
        return carry

    lax.fori_loop(1, devices, greet, 0)
    pl.semaphore_signal(barrier, inc=1, device_id=(1 - slot, me), device_id_type=MESH)

    def part(index):
        return pl.ds(pl.multiple_of(index * block, block), block)

    def exchange(src, dst, m, c, phase, k):
        target = lax.rem(me + k, devices)
        return pltpu.make_async_remote_copy(
            src_ref=src.at[m, c, part(target)],
            dst_ref=dst.at[m, c, part(me)],
            send_sem=a2a_send.at[phase, c, k],
            recv_sem=a2a_recv.at[phase, c, k],
            device_id=(slot, target),
            device_id_type=MESH,
        )

    def start_all(src, dst, m, c, phase):
        def body(k, carry):
            exchange(src, dst, m, c, phase, k).start()
            return carry

        lax.fori_loop(1, devices, body, 0)
        dst[m, c, part(me), :] = src[m, c, part(me), :]

    def wait_all(src, dst, m, c, phase):
        def body(k, carry):
            exchange(src, dst, m, c, phase, k).wait_recv()
            return carry

        lax.fori_loop(1, devices, body, 0)

    def beside(first, count, low, size, put, step, index):
        return pltpu.make_async_remote_copy(
            src_ref=ext.at[pl.ds(first, count), pl.ds(low, size)],
            dst_ref=ext.at[pl.ds(first, count), pl.ds(put, size)],
            send_sem=halo_send.at[index],
            recv_sem=halo_recv.at[index],
            device_id=(slot, lax.rem(me + step, devices)),
            device_id_type=MESH,
        )

    halos = [
        beside(V0, 1, 5, 3, 1, 1, 0),
        beside(V0, 1, 4, 4, 8, devices - 1, 1),
        beside(V1, 1, 5, 3, 1, 1, 2),
        beside(V1, 1, 4, 4, 8, devices - 1, 3),
        beside(S0, 2, 5, 3, 1, 1, 4),
        beside(S0, 2, 4, 4, 8, devices - 1, 5),
        beside(V2, 1, 4, 1, 8, devices - 1, 6),
    ]

    def ahead(src, dst, index):
        return pltpu.make_async_remote_copy(
            src_ref=src,
            dst_ref=dst,
            send_sem=time_send.at[index],
            recv_sem=time_recv.at[index],
            device_id=(1 - slot, me),
            device_id_type=MESH,
        )

    handed = [ahead(recv_b.at[1, c], passed.at[c], c) for c in range(CHUNKS)]
    handed.append(ahead(vb.at[pl.ds(2, 9)], va.at[pl.ds(2, 9)], CHUNKS))
    handed.append(ahead(delta.at[1], delta.at[2], CHUNKS + 1))

    def quad(m, terms):
        w = WEIGHTS[m]
        return 0.5 * (w[0] * terms[0] + w[1] * terms[1] + w[2] * terms[2])

    def old_rates(x):
        return [react(nodes[0, j, x]) + implicit[0, j, x] for j in range(3)]

    def forward(rhs, x, m):
        field = left(by, right(rhs, bzt))
        for c in range(CHUNKS):
            for d in range(size_y // GROUP):
                send_a[m, c, pl.ds(pl.multiple_of(d * block + x * GROUP, GROUP), GROUP), :] = field[
                    d * GROUP : (d + 1) * GROUP, c * LANES : (c + 1) * LANES
                ]

    def backward(chunk, x):
        field = jnp.concatenate(
            [
                jnp.concatenate(
                    [
                        chunk(c, pl.ds(pl.multiple_of(d * block + x * GROUP, GROUP), GROUP))
                        for d in range(size_y // GROUP)
                    ],
                    axis=0,
                )
                for c in range(CHUNKS)
            ],
            axis=1,
        )
        return right(left(byt, field), bz)

    def first_rhs(x, carry):
        rhs = nodes[0, 0, x] - 0.25 * implicit[0, 1, x] + quad(0, old_rates(x))
        out_i[0, 0, x] = rhs
        forward(rhs, x, 0)
        return carry

    lax.fori_loop(0, planes, first_rhs, 0)
    pl.semaphore_wait(barrier, devices)

    def waves(index, size):
        half = size // 2
        freq = jnp.where(index <= half, index, index - half).astype(F32)
        kappa = freq * (2.0 * math.pi / size)
        return kappa * kappa

    def solve_lines(m, c):
        lines = jnp.concatenate(
            [recv_a[m, c, pl.ds(k, size_x, stride=GROUP), :] for k in range(GROUP)], axis=1
        )
        field = left(bxt, left(bx, lines) * factor[c])
        for k in range(GROUP):
            send_b[m, c, pl.ds(k, size_x, stride=GROUP), :] = field[:, k * LANES : (k + 1) * LANES]

    def average(index, value):
        pool[index] = right_exact(value, pz)
        return 0.5 * (
            pool[index, pl.ds(0, size_y // 2, stride=2), :]
            + pool[index, pl.ds(1, size_y // 2, stride=2), :]
        )

    for c in range(CHUNKS):
        start_all(send_a, recv_a, 0, c, 0)

    shape = (size_x, LANES)
    lam_x = waves(lax.broadcasted_iota(jnp.int32, shape, 0), size_x)
    for c in range(CHUNKS):
        lam_z = waves(lax.broadcasted_iota(jnp.int32, shape, 1) + c * LANES, size_z)
        for k in range(GROUP):
            lam_y = waves(jnp.full(shape, me * GROUP + k, jnp.int32), size_y)
            factor[c, :, k * LANES : (k + 1) * LANES] = 1.0 / (1.0 + 0.5 * (lam_x + lam_y + lam_z))

    def pool_start(p, carry):
        ext[V0, 4 + p] = average(0, 0.5 * (nodes[0, 0, 2 * p] + nodes[0, 0, 2 * p + 1]))
        return carry

    lax.fori_loop(0, planes // 2, pool_start, 0)
    halos[0].start()
    halos[1].start()

    def transfer_lines(m):
        for c in range(CHUNKS):
            wait_all(send_a, recv_a, m, c, 2 * m)
            solve_lines(m, c)
            start_all(send_b, recv_b, m, c, 2 * m + 1)

    transfer_lines(0)
    for c in range(CHUNKS):
        wait_all(send_b, recv_b, 0, c, 1)

    def middle(x, carry):
        solved = backward(lambda c, at: recv_b[0, c, at, :], x)
        term = (solved - out_i[0, 0, x]) * 4.0
        out_n[0, 1, x] = solved
        out_i[0, 0, x] = term
        rhs = (
            solved
            + 0.25 * (react(solved) - react(nodes[0, 1, x]))
            - 0.25 * implicit[0, 2, x]
            + quad(1, old_rates(x))
        )
        out_i[0, 1, x] = rhs
        forward(rhs, x, 1)
        return carry

    lax.fori_loop(0, planes, middle, 0)
    for c in range(CHUNKS):
        start_all(send_a, recv_a, 1, c, 2)

    def pool_middle(p, carry):
        ext[V1, 4 + p] = average(0, 0.5 * (out_n[0, 1, 2 * p] + out_n[0, 1, 2 * p + 1]))
        return carry

    lax.fori_loop(0, planes // 2, pool_middle, 0)
    halos[2].start()
    halos[3].start()

    transfer_lines(1)
    for c in range(CHUNKS):
        wait_all(send_b, recv_b, 1, c, 3)

        @pl.when(slot == 0)
        def _():
            handed[c].start()

    def last(p, carry):
        quads = [0.0, 0.0]
        total = 0.0
        for x in (2 * p, 2 * p + 1):
            solved = backward(lambda c, at: recv_b[1, c, at, :], x)
            term = (solved - out_i[0, 1, x]) * 4.0
            out_n[0, 2, x] = solved
            out_i[0, 1, x] = term
            fresh = [
                react(nodes[0, 0, x]) + implicit[0, 0, x],
                react(out_n[0, 1, x]) + out_i[0, 0, x],
                react(solved) + term,
            ]
            quads = [quads[m] + quad(m, fresh) for m in range(2)]
            total = total + solved
        ext[S0, 4 + p] = average(0, 0.5 * quads[0])
        ext[S1, 4 + p] = average(1, 0.5 * quads[1])
        ext[V2, 4 + p] = average(2, 0.5 * total)
        return carry

    lax.fori_loop(0, planes // 2, last, 0)
    for halo in halos[4:]:
        halo.start()
    for halo in halos:
        halo.wait_recv()

    @pl.when(slot == 0)
    def _():
        first = ext[V0, 1:12] + ext[S0, 1:12]
        second = first[1:-1] + 0.25 * (rate(first) - rate(ext[V1, 1:12])) + ext[S1, 2:11]
        vb[2:11] = second
        handed[CHUNKS].start()
        delta[0] = first[3:8] - ext[V1, 4:9]
        delta[1] = second[2:7] - ext[V2, 4:9]
        handed[CHUNKS + 1].start()

    @pl.when(slot == 1)
    def _():
        handed[CHUNKS].wait_recv()
        begin = va[2:11]
        first = begin[1:-1] + 0.25 * (rate(begin) - rate(ext[V0, 2:11])) + ext[S0, 3:10]
        second = first[1:-1] + 0.25 * (rate(first) - rate(ext[V1, 3:10])) + ext[S1, 4:9]
        delta[0] = first[1:6] - ext[V1, 4:9]
        delta[1] = second - ext[V2, 4:9]

    def refined(index):
        def body(p, carry):
            coarse = delta[index, p]
            rows[pl.ds(0, size_y // 2, stride=2), :] = coarse
            rows[pl.ds(1, size_y // 2, stride=2), :] = 0.5 * (
                coarse + pltpu.roll(coarse, size_y // 2 - 1, 0)
            )
            grid[p] = right_exact(rows[...], iz)
            return carry

        lax.fori_loop(0, planes // 2 + 1, body, 0)

    def correct(index, base, target):
        refined(index)

        def body(p, carry):
            out_n[0, target, 2 * p] = base(2 * p) + grid[p]
            out_n[0, target, 2 * p + 1] = base(2 * p + 1) + 0.5 * (grid[p] + grid[p + 1])
            return carry

        lax.fori_loop(0, planes // 2, body, 0)

    correct(0, lambda x: out_n[0, 1, x], 1)
    correct(1, lambda x: out_n[0, 2, x], 2)

    @pl.when(slot == 0)
    def _():
        out_n[0, 0] = nodes[0, 0]
        for copy in handed:
            copy.wait_send()

    @pl.when(slot == 1)
    def _():
        for c in range(CHUNKS):
            handed[c].wait_recv()

        handed[CHUNKS + 1].wait_recv()
        correct(2, lambda x: backward(lambda c, at: passed[c, at, :], x), 0)

    for phase, (src, dst) in enumerate([(send_a, recv_a), (send_b, recv_b)] * 2):
        for c in range(CHUNKS):

            def body(k, carry, src=src, dst=dst, phase=phase, c=c):
                exchange(src, dst, phase // 2, c, phase, k).wait_send()
                return carry

            lax.fori_loop(1, devices, body, 0)
    for halo in halos:
        halo.wait_send()


def fused(fine_nodes, fine_implicit):
    planes, size_y, size_z = fine_nodes.shape[2:]
    devices = lax.axis_size("space")
    basis_x = host_basis(planes * devices)
    basis_y = host_basis(size_y)
    basis_z = host_basis(size_z)
    cells = np.arange(size_z)
    half = np.zeros((size_z, size_z // 2))
    half[cells, cells // 2] = 0.5
    lines = np.zeros((size_z // 2, size_z))
    coarse = np.arange(size_z // 2)
    lines[coarse, 2 * coarse] = 1.0
    lines[coarse, 2 * coarse + 1] += 0.5
    lines[(coarse + 1) % (size_z // 2), 2 * coarse + 1] += 0.5
    constants = [
        two_parts(m) for m in (basis_z, basis_z.T, basis_x, basis_x.T, basis_y, basis_y.T)
    ]
    constants.append(jnp.asarray(half.astype(ml_dtypes.bfloat16)))
    constants.append(jnp.asarray(lines.astype(ml_dtypes.bfloat16)))
    field = (2, CHUNKS, devices * planes * GROUP, LANES)
    plane = (size_y // 2, size_z // 2)
    vmem = pl.BlockSpec(memory_space=pltpu.VMEM)
    shape_n = fine_nodes.shape
    shape_i = shape_n[:1] + (2,) + shape_n[2:]
    return pl.pallas_call(
        kernel,
        out_shape=(jax.ShapeDtypeStruct(shape_n, F32), jax.ShapeDtypeStruct(shape_i, F32)),
        in_specs=[vmem] * 10,
        out_specs=(vmem, vmem),
        scratch_shapes=[
            pltpu.VMEM(field, F32),
            pltpu.VMEM(field, F32),
            pltpu.VMEM(field, F32),
            pltpu.VMEM(field, F32),
            pltpu.VMEM(field[1:], F32),
            pltpu.VMEM((CHUNKS, planes * devices, GROUP * LANES), F32),
            pltpu.VMEM((3, size_y, size_z // 2), F32),
            pltpu.VMEM((5, 12) + plane, F32),
            pltpu.VMEM((12,) + plane, F32),
            pltpu.VMEM((12,) + plane, F32),
            pltpu.VMEM((3, 5) + plane, F32),
            pltpu.VMEM((size_y, size_z // 2), F32),
            pltpu.VMEM((5, size_y, size_z), F32),
            pltpu.SemaphoreType.DMA((4, CHUNKS, devices)),
            pltpu.SemaphoreType.DMA((4, CHUNKS, devices)),
            pltpu.SemaphoreType.DMA((7,)),
            pltpu.SemaphoreType.DMA((7,)),
            pltpu.SemaphoreType.DMA((CHUNKS + 2,)),
            pltpu.SemaphoreType.DMA((CHUNKS + 2,)),
        ],
        compiler_params=pltpu.CompilerParams(
            collective_id=0, has_side_effects=True, vmem_limit_bytes=56 * 2**20
        ),
    )(fine_nodes, fine_implicit, *constants)


def either(fine_nodes, fine_implicit):
    planes, size_y, size_z = fine_nodes.shape[2:]
    devices = lax.axis_size("space")
    fits = planes == GROUP and size_y == GROUP * devices and size_z == CHUNKS * LANES
    if fits and lax.axis_size("tm") == 2:
        return fused(fine_nodes, fine_implicit)
    return on_device(fine_nodes, fine_implicit)


def solution(mesh):
    return jax.shard_map(
        either,
        mesh=mesh,
        in_specs=(P("tm", None, "space", None, None), P("tm", None, "space", None, None)),
        out_specs=(P("tm", None, "space", None, None), P("tm", None, "space", None, None)),
        check_vma=False,
    )
```

profile of v0, /device:TPU:31, one launch (start us, length us, event | category | flops | bytes accessed | tf_op | source)
XLA Modules:
  0.0 153.0 jit_solution(6517971227942792110)
XLA Ops:
  0.6 147.0 %shard_map.113 = (f32[1,3,8,128,256]{4,3,2,1,0:T(8,128)}, f32[1,2,8,128,256]{4,3,2,1,0:T(8,128)}) custom-call(f32[1,3,8,128,256]{4,3,2,1,0:T(8,128)} %nodes.1, f32[1,3,8,128,256]{4,3,2,1,0:T(8,128)} %implicit.1, bf16[2,256,256]{2,1,0:T(8,128)(2,1)} %constant.12.clone.bz, bf16[2,256,256]{2,1,0:T(8,128)(2,1)} %constant.13.clone.bzt, ...), custom_call_target="tpu_custom_call" | custom-call | tf_op jit(solution)/shard_map/pallas_call | solution.py:584
  147.7 0.0 copy-start
  147.7 4.0 %copy.14 = f32[1,3,8,128,256]{4,3,2,1,0:T(8,128)} copy(f32[1,3,8,128,256]{4,3,2,1,0:T(8,128)} %get-tuple-element.4) | data formatting | bytes 6291456
  151.7 0.0 copy-done
  151.7 1.3 copy.15
Async XLA Ops:
  147.7 4.0 %copy-start = (f32[1,2,8,128,256]{4,3,2,1,0:T(8,128)S(1)}, f32[1,2,8,128,256]{4,3,2,1,0:T(8,128)}, u32[]{:S(2)}) copy-start(f32[1,2,8,128,256]{4,3,2,1,0:T(8,128)} %get-tuple-element.5) | copy-start | bytes 6291460
where the time goes:
time: 153 us
  Pallas kernels  147 us (96%)
  local copies, waits for them, and re-layouts  5.33 us (3%)
    pallas_call x1, Pallas kernels, fused(): pl.pallas_call(kernel, out_shape=(jax.ShapeDtypeStruct(shape_n, F32), jax...  147 us
    unnamed x4, local copies, waits for them, and re-layouts  5.33 us

commit v1 on v0

--- a/solution.py
+++ b/solution.py
@@ -252,7 +252,7 @@
 def kernel(
     nodes, implicit, bz, bzt, bx, bxt, by, byt, pz, iz,
     out_n, out_i,
-    send_a, recv_a, send_b, recv_b, passed, factor, pool, ext, va, vb, delta, rows, grid,
+    send_a, recv_a, send_b, recv_b, passed, factor, pool, ext, va, vb, delta, rows, grid, early,
     a2a_send, a2a_recv, halo_send, halo_recv, time_send, time_recv,
 ):
     slot = lax.axis_index("tm")
@@ -351,21 +351,27 @@
                     d * GROUP : (d + 1) * GROUP, c * LANES : (c + 1) * LANES
                 ]
 
+    def undo(chunk, c, x):
+        return left(
+            byt,
+            jnp.concatenate(
+                [
+                    chunk(c, pl.ds(pl.multiple_of(d * block + x * GROUP, GROUP), GROUP))
+                    for d in range(size_y // GROUP)
+                ],
+                axis=0,
+            ),
+        )
+
+    def prepare(chunk):
+        def body(x, carry):
+            early[x] = undo(chunk, 0, x)
+            return carry
+
+        lax.fori_loop(0, planes, body, 0, unroll=4)
+
     def backward(chunk, x):
-        field = jnp.concatenate(
-            [
-                jnp.concatenate(
-                    [
-                        chunk(c, pl.ds(pl.multiple_of(d * block + x * GROUP, GROUP), GROUP))
-                        for d in range(size_y // GROUP)
-                    ],
-                    axis=0,
-                )
-                for c in range(CHUNKS)
-            ],
-            axis=1,
-        )
-        return right(left(byt, field), bz)
+        return right(jnp.concatenate([early[x], undo(chunk, 1, x)], axis=1), bz)
 
     def first_rhs(x, carry):
         rhs = nodes[0, 0, x] - 0.25 * implicit[0, 1, x] + quad(0, old_rates(x))
@@ -373,7 +379,7 @@
         forward(rhs, x, 0)
         return carry
 
-    lax.fori_loop(0, planes, first_rhs, 0)
+    lax.fori_loop(0, planes, first_rhs, 0, unroll=4)
     pl.semaphore_wait(barrier, devices)
 
     def waves(index, size):
@@ -425,6 +431,8 @@
     transfer_lines(0)
     for c in range(CHUNKS):
         wait_all(send_b, recv_b, 0, c, 1)
+        if c == 0:
+            prepare(lambda c, at: recv_b[0, c, at, :])
 
     def middle(x, carry):
         solved = backward(lambda c, at: recv_b[0, c, at, :], x)
@@ -441,7 +449,7 @@
         forward(rhs, x, 1)
         return carry
 
-    lax.fori_loop(0, planes, middle, 0)
+    lax.fori_loop(0, planes, middle, 0, unroll=4)
     for c in range(CHUNKS):
         start_all(send_a, recv_a, 1, c, 2)
 
@@ -460,6 +468,9 @@
         @pl.when(slot == 0)
         def _():
             handed[c].start()
+
+        if c == 0:
+            prepare(lambda c, at: recv_b[1, c, at, :])
 
     def last(p, carry):
         quads = [0.0, 0.0]
@@ -481,7 +492,7 @@
         ext[V2, 4 + p] = average(2, 0.5 * total)
         return carry
 
-    lax.fori_loop(0, planes // 2, last, 0)
+    lax.fori_loop(0, planes // 2, last, 0, unroll=2)
     for halo in halos[4:]:
         halo.start()
     for halo in halos:
@@ -526,7 +537,7 @@
             out_n[0, target, 2 * p + 1] = base(2 * p + 1) + 0.5 * (grid[p] + grid[p + 1])
             return carry
 
-        lax.fori_loop(0, planes // 2, body, 0)
+        lax.fori_loop(0, planes // 2, body, 0, unroll=2)
 
     correct(0, lambda x: out_n[0, 1, x], 1)
     correct(1, lambda x: out_n[0, 2, x], 2)
@@ -541,6 +552,8 @@
     def _():
         for c in range(CHUNKS):
             handed[c].wait_recv()
+            if c == 0:
+                prepare(lambda c, at: passed[c, at, :])
 
         handed[CHUNKS + 1].wait_recv()
         correct(2, lambda x: backward(lambda c, at: passed[c, at, :], x), 0)
@@ -600,6 +613,7 @@
             pltpu.VMEM((3, 5) + plane, F32),
             pltpu.VMEM((size_y, size_z // 2), F32),
             pltpu.VMEM((5, size_y, size_z), F32),
+            pltpu.VMEM((planes, size_y, LANES), F32),
             pltpu.SemaphoreType.DMA((4, CHUNKS, devices)),
             pltpu.SemaphoreType.DMA((4, CHUNKS, devices)),
             pltpu.SemaphoreType.DMA((7,)),

time: 153 us -> 149 us (0.974)
  Pallas kernels: 147 us -> 143 us
    pallas_call x1, Pallas kernels: 147 us -> 143 us  [fused(): pl.pallas_call(kernel, out_shape=(jax.ShapeDtypeStruct(shape_n, F32), jax...]
where the time goes in v1:
time: 149 us
  Pallas kernels  143 us (96%)
  local copies, waits for them, and re-layouts  5.33 us (4%)
    pallas_call x1, Pallas kernels, fused(): pl.pallas_call(kernel, out_shape=(jax.ShapeDtypeStruct(shape_n, F32), jax...  143 us
    unnamed x4, local copies, waits for them, and re-layouts  5.33 us

profile of v1, /device:TPU:31, one launch (start us, length us, event | category | flops | bytes accessed | tf_op | source)
XLA Modules:
  0.0 148.7 jit_solution(63058080313424941)
XLA Ops:
  0.6 142.7 %shard_map.113 = (f32[1,3,8,128,256]{4,3,2,1,0:T(8,128)}, f32[1,2,8,128,256]{4,3,2,1,0:T(8,128)}) custom-call(f32[1,3,8,128,256]{4,3,2,1,0:T(8,128)} %nodes.1, f32[1,3,8,128,256]{4,3,2,1,0:T(8,128)} %implicit.1, bf16[2,256,256]{2,1,0:T(8,128)(2,1)} %constant.12.clone.bz, bf16[2,256,256]{2,1,0:T(8,128)(2,1)} %constant.13.clone.bzt, ...), custom_call_target="tpu_custom_call" | custom-call | tf_op jit(solution)/shard_map/pallas_call | solution.py:597
  143.3 0.0 copy-start
  143.4 4.0 %copy.14 = f32[1,3,8,128,256]{4,3,2,1,0:T(8,128)} copy(f32[1,3,8,128,256]{4,3,2,1,0:T(8,128)} %get-tuple-element.4) | data formatting | bytes 6291456
  147.4 0.0 copy-done
  147.4 1.3 copy.15
Async XLA Ops:
  143.3 4.0 %copy-start = (f32[1,2,8,128,256]{4,3,2,1,0:T(8,128)S(1)}, f32[1,2,8,128,256]{4,3,2,1,0:T(8,128)}, u32[]{:S(2)}) copy-start(f32[1,2,8,128,256]{4,3,2,1,0:T(8,128)} %get-tuple-element.5) | copy-start | bytes 6291460

commit v2 on v1

--- a/solution.py
+++ b/solution.py
@@ -253,7 +253,7 @@
     nodes, implicit, bz, bzt, bx, bxt, by, byt, pz, iz,
     out_n, out_i,
     send_a, recv_a, send_b, recv_b, passed, factor, pool, ext, va, vb, delta, rows, grid, early,
-    a2a_send, a2a_recv, halo_send, halo_recv, time_send, time_recv,
+    a2a_send, a2a_recv, halo_send, halo_recv, time_send, time_recv, piece_send, piece_recv,
 ):
     slot = lax.axis_index("tm")
     me = lax.axis_index("space")
@@ -332,9 +332,21 @@
             device_id_type=MESH,
         )
 
-    handed = [ahead(recv_b.at[1, c], passed.at[c], c) for c in range(CHUNKS)]
-    handed.append(ahead(vb.at[pl.ds(2, 9)], va.at[pl.ds(2, 9)], CHUNKS))
-    handed.append(ahead(delta.at[1], delta.at[2], CHUNKS + 1))
+    handed = [
+        ahead(vb.at[pl.ds(2, 9)], va.at[pl.ds(2, 9)], 0),
+        ahead(delta.at[1], delta.at[2], 1),
+    ]
+
+    def piece(c, k):
+        source = lax.rem(me + devices - k, devices)
+        return pltpu.make_async_remote_copy(
+            src_ref=recv_b.at[1, c, part(source)],
+            dst_ref=passed.at[c, part(source)],
+            send_sem=piece_send.at[c, k],
+            recv_sem=piece_recv.at[c, k],
+            device_id=(1 - slot, me),
+            device_id_type=MESH,
+        )
 
     def quad(m, terms):
         w = WEIGHTS[m]
@@ -379,7 +391,7 @@
         forward(rhs, x, 0)
         return carry
 
-    lax.fori_loop(0, planes, first_rhs, 0, unroll=4)
+    lax.fori_loop(0, planes, first_rhs, 0, unroll=8)
     pl.semaphore_wait(barrier, devices)
 
     def waves(index, size):
@@ -449,7 +461,7 @@
         forward(rhs, x, 1)
         return carry
 
-    lax.fori_loop(0, planes, middle, 0, unroll=4)
+    lax.fori_loop(0, planes, middle, 0, unroll=8)
     for c in range(CHUNKS):
         start_all(send_a, recv_a, 1, c, 2)
 
@@ -463,11 +475,20 @@
 
     transfer_lines(1)
     for c in range(CHUNKS):
-        wait_all(send_b, recv_b, 1, c, 3)
-
         @pl.when(slot == 0)
         def _():
-            handed[c].start()
+            piece(c, 0).start()
+
+        def arrive(k, carry):
+            exchange(send_b, recv_b, 1, c, 3, k).wait_recv()
+
+            @pl.when(slot == 0)
+            def _():
+                piece(c, k).start()
+
+            return carry
+
+        lax.fori_loop(1, devices, arrive, 0)
 
         if c == 0:
             prepare(lambda c, at: recv_b[1, c, at, :])
@@ -492,7 +513,7 @@
         ext[V2, 4 + p] = average(2, 0.5 * total)
         return carry
 
-    lax.fori_loop(0, planes // 2, last, 0, unroll=2)
+    lax.fori_loop(0, planes // 2, last, 0, unroll=4)
     for halo in halos[4:]:
         halo.start()
     for halo in halos:
@@ -503,14 +524,14 @@
         first = ext[V0, 1:12] + ext[S0, 1:12]
         second = first[1:-1] + 0.25 * (rate(first) - rate(ext[V1, 1:12])) + ext[S1, 2:11]
         vb[2:11] = second
-        handed[CHUNKS].start()
+        handed[0].start()
         delta[0] = first[3:8] - ext[V1, 4:9]
         delta[1] = second[2:7] - ext[V2, 4:9]
-        handed[CHUNKS + 1].start()
+        handed[1].start()
 
     @pl.when(slot == 1)
     def _():
-        handed[CHUNKS].wait_recv()
+        handed[0].wait_recv()
         begin = va[2:11]
         first = begin[1:-1] + 0.25 * (rate(begin) - rate(ext[V0, 2:11])) + ext[S0, 3:10]
         second = first[1:-1] + 0.25 * (rate(first) - rate(ext[V1, 3:10])) + ext[S1, 4:9]
@@ -520,14 +541,14 @@
     def refined(index):
         def body(p, carry):
             coarse = delta[index, p]
-            rows[pl.ds(0, size_y // 2, stride=2), :] = coarse
-            rows[pl.ds(1, size_y // 2, stride=2), :] = 0.5 * (
+            rows[p, pl.ds(0, size_y // 2, stride=2), :] = coarse
+            rows[p, pl.ds(1, size_y // 2, stride=2), :] = 0.5 * (
                 coarse + pltpu.roll(coarse, size_y // 2 - 1, 0)
             )
-            grid[p] = right_exact(rows[...], iz)
+            grid[p] = right_exact(rows[p], iz)
             return carry
 
-        lax.fori_loop(0, planes // 2 + 1, body, 0)
+        lax.fori_loop(0, planes // 2 + 1, body, 0, unroll=True)
 
     def correct(index, base, target):
         refined(index)
@@ -547,15 +568,27 @@
         out_n[0, 0] = nodes[0, 0]
         for copy in handed:
             copy.wait_send()
+        for c in range(CHUNKS):
+
+            def left_here(k, carry, c=c):
+                piece(c, k).wait_send()
+                return carry
+
+            lax.fori_loop(0, devices, left_here, 0)
 
     @pl.when(slot == 1)
     def _():
         for c in range(CHUNKS):
-            handed[c].wait_recv()
+
+            def landed(k, carry, c=c):
+                piece(c, k).wait_recv()
+                return carry
+
+            lax.fori_loop(0, devices, landed, 0)
             if c == 0:
                 prepare(lambda c, at: passed[c, at, :])
 
-        handed[CHUNKS + 1].wait_recv()
+        handed[1].wait_recv()
         correct(2, lambda x: backward(lambda c, at: passed[c, at, :], x), 0)
 
     for phase, (src, dst) in enumerate([(send_a, recv_a), (send_b, recv_b)] * 2):
@@ -611,15 +644,17 @@
             pltpu.VMEM((12,) + plane, F32),
             pltpu.VMEM((12,) + plane, F32),
             pltpu.VMEM((3, 5) + plane, F32),
-            pltpu.VMEM((size_y, size_z // 2), F32),
+            pltpu.VMEM((5, size_y, size_z // 2), F32),
             pltpu.VMEM((5, size_y, size_z), F32),
             pltpu.VMEM((planes, size_y, LANES), F32),
             pltpu.SemaphoreType.DMA((4, CHUNKS, devices)),
             pltpu.SemaphoreType.DMA((4, CHUNKS, devices)),
             pltpu.SemaphoreType.DMA((7,)),
             pltpu.SemaphoreType.DMA((7,)),
-            pltpu.SemaphoreType.DMA((CHUNKS + 2,)),
-            pltpu.SemaphoreType.DMA((CHUNKS + 2,)),
+            pltpu.SemaphoreType.DMA((2,)),
+            pltpu.SemaphoreType.DMA((2,)),
+            pltpu.SemaphoreType.DMA((CHUNKS, devices)),
+            pltpu.SemaphoreType.DMA((CHUNKS, devices)),
         ],
         compiler_params=pltpu.CompilerParams(
             collective_id=0, has_side_effects=True, vmem_limit_bytes=56 * 2**20

time: 149 us -> 144 us (0.966)
  Pallas kernels: 143 us -> 137 us
    pallas_call x1, Pallas kernels: 143 us -> 137 us  [fused(): pl.pallas_call(kernel, out_shape=(jax.ShapeDtypeStruct(shape_n, F32), jax...]
where the time goes in v2:
time: 144 us; the launch traced here: 143 us
  Pallas kernels  137 us (95%)
  local copies, waits for them, and re-layouts  5.33 us (4%)
    pallas_call x1, Pallas kernels, fused(): pl.pallas_call(kernel, out_shape=(jax.ShapeDtypeStruct(shape_n, F32), jax...  137 us
    unnamed x4, local copies, waits for them, and re-layouts  5.33 us

profile of v2, /device:TPU:31, one launch (start us, length us, event | category | flops | bytes accessed | tf_op | source)
XLA Modules:
  0.0 142.7 jit_solution(7462095625294771070)
XLA Ops:
  0.6 136.8 %shard_map.113 = (f32[1,3,8,128,256]{4,3,2,1,0:T(8,128)}, f32[1,2,8,128,256]{4,3,2,1,0:T(8,128)}) custom-call(f32[1,3,8,128,256]{4,3,2,1,0:T(8,128)} %nodes.1, f32[1,3,8,128,256]{4,3,2,1,0:T(8,128)} %implicit.1, bf16[2,256,256]{2,1,0:T(8,128)(2,1)} %constant.12.clone.bz, bf16[2,256,256]{2,1,0:T(8,128)(2,1)} %constant.13.clone.bzt, ...), custom_call_target="tpu_custom_call" | custom-call | tf_op jit(solution)/shard_map/pallas_call | solution.py:630
  137.4 0.0 copy-start
  137.4 4.0 %copy.14 = f32[1,3,8,128,256]{4,3,2,1,0:T(8,128)} copy(f32[1,3,8,128,256]{4,3,2,1,0:T(8,128)} %get-tuple-element.4) | data formatting | bytes 6291456
  141.4 0.0 copy-done
  141.4 1.3 copy.15
Async XLA Ops:
  137.4 4.0 %copy-start = (f32[1,2,8,128,256]{4,3,2,1,0:T(8,128)S(1)}, f32[1,2,8,128,256]{4,3,2,1,0:T(8,128)}, u32[]{:S(2)}) copy-start(f32[1,2,8,128,256]{4,3,2,1,0:T(8,128)} %get-tuple-element.5) | copy-start | bytes 6291460
